TPU v7x, 256 devices: a whole 4x4x8 slice. The times are simulated.
256 devices in a mesh: dp: 8 (over y, core), lang: 32 (over x, z).
Axes of the slice: x: 4, y: 4, z: 8, core: 2. Of those that a mesh axis runs over, the one named last changes fastest.
Arguments:
- inputs: bfloat16 [32768, 2048], P(('dp', 'lang')), may hold values from -6 to 6
- grad_out: bfloat16 [32768, 2048], P(('dp', 'lang')), may hold values from -6 to 6
- lang_ids: int32 [32768], P(('dp', 'lang')), may hold values from 0 to 199, as said below
- lang_block: int32 [200], replicated, may hold values from 0 to 31, as said below
- block_owner: int32 [32], replicated, may hold values from 0 to 31, each once
- w_in: bfloat16 [32, 4096, 2048], P('lang', 'dp'), may hold values from -0.125 to 0.125
- w_out: bfloat16 [32, 4096, 2048], P('lang', 'dp'), may hold values from -0.09375 to 0.09375
Outputs:
- grad_in: bfloat16 [32768, 2048], P(('dp', 'lang'))
- grad_w_in: bfloat16 [32, 4096, 2048], P('lang', 'dp')
- grad_w_out: bfloat16 [32, 4096, 2048], P('lang', 'dp')
Inputs may be any that keep to these rules, and one draw needn't show every extreme that they name: `lang_ids`: through lang_block, the 128 rows of one device name any one block at most 5 times; in every draw one block is named exactly 5 times by the rows of every device. `lang_block`: every block has at least one language. A permutation: block b's weights and gradients sit at index block_owner[b] of the block dimension.
All inputs are finite; a program needn't handle non-finite values.
Results may differ from a plain program's by a relative error of at most 0.019.
Values may be sent and summed in bfloat16 or wider, within the bound.
A program may use at most 128 MiB of HBM per device.

v0:
```python
import math
import jax
import jax.numpy as jnp
from jax import lax
from jax.sharding import PartitionSpec as P

gelu_scale = math.sqrt(2.0 / math.pi)


def gelu_parts(pre_act):
    tanh_arg = gelu_scale * (pre_act + 0.044715 * pre_act * pre_act * pre_act)
    tangent = jnp.tanh(tanh_arg)
    gelu_value = 0.5 * pre_act * (1.0 + tangent)
    gelu_slope = 0.5 * (1.0 + tangent) + 0.5 * pre_act * (1.0 - tangent * tangent) * gelu_scale * (
        1.0 + 3.0 * 0.044715 * pre_act * pre_act
    )
    return (gelu_value, gelu_slope)


def local_grads(gathered, w_first, w_second):
    rows_x = gathered[:, 0]
    rows_g = gathered[:, 1]
    pre_act = jnp.dot(rows_x, w_first.T, preferred_element_type=jnp.float32)
    gelu_value, gelu_slope = gelu_parts(pre_act)
    activated = gelu_value.astype(jnp.bfloat16)
    back_grad = jnp.dot(rows_g, w_second.T, preferred_element_type=jnp.float32)
    pre_grad = (back_grad * gelu_slope).astype(jnp.bfloat16)
    g_out = jnp.dot(activated.T, rows_g, preferred_element_type=jnp.float32).astype(jnp.bfloat16)
    g_in = jnp.dot(pre_grad.T, rows_x, preferred_element_type=jnp.float32).astype(jnp.bfloat16)
    return (pre_grad, g_in, g_out)


def body(inputs, grad_out, lang_ids, lang_block, block_owner, w_in, w_out):
    tok_rows = inputs.shape[0]
    feat_width = inputs.shape[1]
    lang_count = lax.axis_size("lang")
    dp_count = lax.axis_size("dp")
    per_peer = 5 * tok_rows // (4 * lang_count)
    languages = lang_block.shape[0]
    block_count = block_owner.shape[0]
    lang_hits = (lang_ids[:, None] == jnp.arange(languages, dtype=jnp.int32)[None, :]).astype(
        jnp.int32
    )
    row_block = jnp.sum(lang_hits * lang_block[None, :], axis=1)
    block_hits = (row_block[:, None] == jnp.arange(block_count, dtype=jnp.int32)[None, :]).astype(
        jnp.int32
    )
    holder = jnp.sum(block_hits * block_owner[None, :], axis=1)
    holder_hits = (holder[:, None] == jnp.arange(lang_count, dtype=jnp.int32)[None, :]).astype(
        jnp.int32
    )
    earlier = jnp.cumsum(holder_hits, axis=0) - holder_hits
    slot_index = jnp.sum(earlier * holder_hits, axis=1)
    position = holder * per_peer + slot_index
    packed = jnp.stack([inputs, grad_out], axis=1)
    w_first = w_in[0]
    w_second = w_out[0]
    col_rows, col_pos = (
        lax.all_gather(packed[None], "dp", axis=0, tiled=True),
        lax.all_gather(position[None], "dp", axis=0, tiled=True),
    )
    dp_index = jnp.arange(dp_count, dtype=jnp.int32)[:, None]
    target = col_pos // per_peer * (dp_count * per_peer) + dp_index * per_peer + col_pos % per_peer
    outgoing = jnp.zeros((lang_count * dp_count * per_peer, 2, feat_width), jnp.bfloat16)
    outgoing = outgoing.at[target.reshape(-1)].set(col_rows.reshape(-1, 2, feat_width), mode="drop")
    arrived = lax.all_to_all(
        outgoing.reshape(lang_count, dp_count * per_peer, 2, feat_width),
        "lang",
        split_axis=0,
        concat_axis=0,
        tiled=True,
    )
    gathered = arrived.reshape(-1, 2, feat_width)
    pre_grad, g_in, g_out = local_grads(gathered, w_first, w_second)
    partial_dx = jnp.dot(pre_grad, w_first, preferred_element_type=jnp.float32)
    partial_dx = partial_dx.reshape(lang_count, dp_count, per_peer, feat_width)
    summed = (
        lax.psum_scatter(partial_dx.astype(jnp.bfloat16), "dp", scatter_dimension=1, tiled=True)
        .astype(jnp.float32)
        .reshape(lang_count, per_peer, feat_width)
    )
    returned = lax.all_to_all(
        summed.astype(jnp.bfloat16), "lang", split_axis=0, concat_axis=0, tiled=True
    )
    grad_in = returned.reshape(lang_count * per_peer, feat_width)[position]
    return (grad_in, g_in[None], g_out[None])


def solution(mesh):
    in_specs = (
        P(("dp", "lang"), None),
        P(("dp", "lang"), None),
        P(("dp", "lang")),
        P(),
        P(),
        P("lang", "dp", None),
        P("lang", "dp", None),
    )
    out_specs = (P(("dp", "lang"), None), P("lang", "dp", None), P("lang", "dp", None))
    return jax.shard_map(body, mesh=mesh, in_specs=in_specs, out_specs=out_specs, check_vma=False)
```

profile of v0, /device:TPU:25, one launch (start us, length us, event | category | flops | bytes accessed | tf_op | source)
XLA Modules:
  0.0 580.1 jit_solution(14757968906127118816)
XLA Ops:
  7.2 0.0 copy-start
  7.2 0.0 copy-start.2
  7.2 0.0 copy-start.3
  7.2 0.0 copy-start.5
  7.2 0.0 all-gather.5.cloned.1.call-start
  7.3 2.4 pad_maximum_fusion
  9.7 0.0 all-gather.5.cloned.1.call-update
  9.7 0.0 reduce-scatter.2.cloned.1.call-start
  9.7 0.0 copy-done.2
  9.7 0.0 copy-done.3
  9.8 0.1 select_reduce_fusion
  9.9 0.0 copy-done.5
  9.9 0.2 select_reduce_fusion.2
  10.0 0.1 fusion.23
  10.1 0.2 reduce_window_sum.11
  10.3 0.2 select_reduce_fusion.1
  10.5 9.0 %all-gather.2 = s32[8,1,128]{2,1,0:T(1,128)S(1)} all-gather(s32[1,1,128]{2,1,0:T(1,128)S(1)} %fusion.34), channel_id=2, replica_groups=mesh['dp'=8,'lang'=32] {'dp'}, dimensions={0}, use_global_device_ids=true | all-gather | bytes 4608 | tf_op jit(solution)/shard_map/all_gather | solution.py:60
  19.5 0.4 rem.15
  19.8 0.1 fusion.26
  19.9 44.1 %all-gather.5.cloned.1.call-done = bf16[1024,2,2048]{2,0,1:T(8,128)(2,1)} async-done(((bf16[128,2,2048]{2,0,1:T(8,128)(2,1)}), bf16[1024,2,2048]{2,0,1:T(8,128)(2,1)}) %all-gather.5.cloned.1.call-update) | async-done | bytes 8388624 | tf_op jit(solution)/shard_map/all_gather | solution.py:59
  64.0 16.4 %copy.33 = bf16[1024,2,2048]{2,1,0:T(2,128)(2,1)} copy(bf16[1024,2,2048]{2,0,1:T(8,128)(2,1)} %all-gather.5.cloned.1.call-done) | data formatting | bytes 16777216 | tf_op jit(solution)/shard_map/all_gather | solution.py:59
  80.4 6.6 %broadcast_in_dim.8 = bf16[1280,2,2048]{2,1,0:T(2,128)(2,1)} broadcast(bf16[]{:T(256)} %constant.15.clone.1), dimensions={} | broadcast | bytes 10485762 | tf_op jit(solution)/shard_map/broadcast_in_dim | solution.py:64
  87.0 127.9 %scatter_fusion = bf16[1280,2,2048]{2,1,0:T(2,128)(2,1)} fusion(bf16[1280,2,2048]{2,1,0:T(2,128)(2,1)} %broadcast_in_dim.8, s32[1024]{0:T(1024)S(1)} %bitcast.74, bf16[1024,2,2048]{2,1,0:T(2,128)(2,1)} %copy.33), kind=kCustom, calls=%fused_computation.1 | custom fusion | bytes 25169920 | tf_op jit(solution)/shard_map/scatter | solution.py:65
  214.9 237.2 %all_to_all.10 = bf16[32,40,2,2048]{3,2,1,0:T(2,128)(2,1)} all-to-all(bf16[32,40,2,2048]{3,2,1,0:T(2,128)(2,1)} %bitcast.62), channel_id=1, replica_groups=mesh['dp'=8,'lang'=32] {'lang'}, dimensions={0} | all-to-all | bytes 20971520 | tf_op jit(solution)/shard_map/all_to_all | solution.py:66
  452.1 12.9 %copy.34 = bf16[32,40,2,2048]{3,1,0,2:T(8,128)(2,1)} copy(bf16[32,40,2,2048]{3,2,1,0:T(2,128)(2,1)} %all_to_all.10) | data formatting | bytes 20971520 | tf_op jit(solution)/shard_map/all_to_all | solution.py:66
  465.0 0.0 copy-done
  465.0 0.0 copy-start.1
  465.0 0.0 copy-start.4
  465.0 5.2 fusion.3
  470.2 0.0 copy-start.6
  470.3 1.5 copy-done.6
  471.7 0.0 copy-done.1
  471.7 0.0 copy-done.4
  471.7 4.3 fusion.5
  476.0 1.6 dot_general.19
  477.6 4.9 convolution_convert_fusion
  482.5 5.2 copy.36
  487.8 0.0 reduce-scatter.2.cloned.1.call-update
  487.8 42.7 %reduce-scatter.2.cloned.1.call-done = bf16[32,1,5,2048]{3,0,2,1:T(8,128)(2,1)} async-done(((bf16[32,8,5,2048]{3,0,2,1:T(8,128)(2,1)}), bf16[32,1,5,2048]{3,0,2,1:T(8,128)(2,1)}) %reduce-scatter.2.cloned.1.call-update) | async-done | bytes 655376 | tf_op jit(solution)/shard_map/reduce_scatter | solution.py:78
  530.5 2.4 copy.37
  532.9 9.6 %all-to-all-start.1 = ((bf16[32,5,2048]{2,1,0:T(8,128)(2,1)}), bf16[32,5,2048]{2,1,0:T(8,128)(2,1)}, u32[]{:S(2)}, u32[]{:S(2)}) async-start(bf16[32,5,2048]{2,1,0:T(8,128)(2,1)} %copy.37), calls=%async_computation.2 | async-start | bytes 2097152 | tf_op jit(solution)/shard_map/all_to_all | solution.py:82
  542.5 0.0 copy-start.7
  542.6 6.7 %fusion.9 = bf16[1,512,2048]{2,1,0:T(8,128)(2,1)} fusion(bf16[1280,512]{1,0:T(8,128)(2,1)S(1)} %fusion.5, bf16[1280,2,2048]{2,0,1:T(8,128)(2,1)} %bitcast.64), kind=kOutput, calls=%fused_computation.16 | convolution fusion | flops 2685403136 | bytes 8650752 | tf_op jit(solution)/shard_map/dot_general | solution.py:29
  549.3 0.0 copy-done.7
  549.3 6.8 %fusion.8 = bf16[1,512,2048]{2,1,0:T(8,128)(2,1)} fusion(bf16[1280,2,2048]{2,0,1:T(8,128)(2,1)} %bitcast.65, f32[1280,512]{1,0:T(8,128)S(1)} %copy-done.7), kind=kOutput, calls=%fused_computation.15 | convolution fusion | flops 2691301376 | bytes 9961472 | tf_op jit(solution)/shard_map/dot_general | solution.py:28
  556.1 14.0 %all-to-all-done.1 = bf16[32,5,2048]{2,1,0:T(8,128)(2,1)} async-done(((bf16[32,5,2048]{2,1,0:T(8,128)(2,1)}), bf16[32,5,2048]{2,1,0:T(8,128)(2,1)}, u32[]{:S(2)}, u32[]{:S(2)}) %all-to-all-start.1) | async-done | bytes 655392 | tf_op jit(solution)/shard_map/all_to_all | solution.py:82
  570.1 1.5 reshape.110
  571.5 1.7 gather_fusion
  (6 shorter events, 0.0 us)
Async XLA Ops:
  7.2 457.8 %copy-start = (bf16[1,512,2048]{2,1,0:T(8,128)(2,1)S(1)}, bf16[1,512,2048]{2,1,0:T(8,128)(2,1)}, u32[]{:S(2)}) copy-start(bf16[1,512,2048]{2,1,0:T(8,128)(2,1)} %param.12) | copy-start | bytes 6291460
  7.2 2.6 copy-start.2
  7.2 2.6 copy-start.3
  7.2 2.7 copy-start.5
  7.2 56.8 %all-gather.5.cloned.1.call-start = ((), (), s32[]{:S(2)}) async-start(), calls=%async_computation.4 | async-start | bytes 9437184 | tf_op jit(solution)/shard_map/all_gather | solution.py:59
  9.7 520.8 %reduce-scatter.2.cloned.1.call-start = ((), (), s32[]{:S(2)}) async-start(), calls=%async_computation.3 | async-start | bytes 5898240 | tf_op jit(solution)/shard_map/reduce_scatter | solution.py:78
  465.0 6.7 %copy-start.1 = (bf16[32,40,2,2048]{3,1,0,2:T(8,128)(2,1)S(1)}, bf16[32,40,2,2048]{3,1,0,2:T(8,128)(2,1)}, u32[]{:S(2)}) copy-start(bf16[32,40,2,2048]{3,1,0,2:T(8,128)(2,1)} %copy.34) | copy-start | bytes 31457284
  465.0 6.7 %copy-start.4 = (bf16[1,512,2048]{2,1,0:T(8,128)(2,1)S(1)}, bf16[1,512,2048]{2,1,0:T(8,128)(2,1)}, u32[]{:S(2)}) copy-start(bf16[1,512,2048]{2,1,0:T(8,128)(2,1)} %param.13) | copy-start | bytes 6291460
  470.2 1.5 copy-start.6
  532.9 37.2 %all-to-all-start.1 = ((bf16[32,5,2048]{2,1,0:T(8,128)(2,1)}), bf16[32,5,2048]{2,1,0:T(8,128)(2,1)}, u32[]{:S(2)}, u32[]{:S(2)}) async-start(bf16[32,5,2048]{2,1,0:T(8,128)(2,1)} %copy.37), calls=%async_computation.2 | async-start | bytes 2097152 | tf_op jit(solution)/shard_map/all_to_all | solution.py:82
  542.5 6.8 %copy-start.7 = (f32[1280,512]{1,0:T(8,128)S(1)}, f32[1280,512]{1,0:T(8,128)}, u32[]{:S(2)}) copy-start(f32[1280,512]{1,0:T(8,128)} %copy-done.6) | copy-start | bytes 7864324
Sparse Core Ops, SparseCore 0:
  10.5 53.4 all-gather.4
  487.9 42.5 reduce-scatter.1
where the time goes:
time: 582 us; the launch traced here: 580 us
  blocking collectives  246 us (42%)
  local copies, waits for them, and re-layouts  178 us (31%)
  waiting for transfers between devices  101 us (17%)
  matrix products  28 us (5%)
  between operations  14.2 us (2%)
  starting transfers between devices  9.69 us (2%)
    all_to_all x1, blocking collectives, body(): lax.all_to_all(outgoing.reshape(lang_count, dp_count * per_peer, 2, feat_...  237 us
    scatter x1, local copies, waits for them, and re-layouts, body(): outgoing.at[target.reshape(-1)]  128 us
    all_gather x1, waiting for transfers between devices, body(): lax.all_gather(packed[None], 'dp', axis=0, tiled=True)  44.1 us
    reduce_scatter x1, waiting for transfers between devices, body(): lax.psum_scatter(partial_dx.astype(jnp.bfloat16), 'dp', scatter_dimension...  42.7 us
    all_gather x1, local copies, waits for them, and re-layouts, body(): lax.all_gather(packed[None], 'dp', axis=0, tiled=True)  16.4 us
    all_to_all x1, waiting for transfers between devices, body(): lax.all_to_all(summed.astype(jnp.bfloat16), 'lang', split_axis=0, concat_...  14 us
    all_to_all x1, local copies, waits for them, and re-layouts, body(): lax.all_to_all(outgoing.reshape(lang_count, dp_count * per_peer, 2, feat_...  12.9 us
  transfers between devices with their start and end apart: 3, of which 3 were waited for; matrix products, arithmetic and copies ran while one was open for 3% of the time, Pallas kernels for 0%

commit v1 on v0

--- a/solution.py
+++ b/solution.py
@@ -5,6 +5,11 @@
 from jax.sharding import PartitionSpec as P
 
 gelu_scale = math.sqrt(2.0 / math.pi)
+
+
+def _step_on_sides(local_x):
+    spare = lax.all_to_all(jnp.stack(lax.psum(1, "dp") * [local_x], axis=0), "dp", 0, 0)
+    return jnp.concatenate(spare, axis=0)
 
 
 def gelu_parts(pre_act):
@@ -56,7 +61,7 @@
     w_first = w_in[0]
     w_second = w_out[0]
     col_rows, col_pos = (
-        lax.all_gather(packed[None], "dp", axis=0, tiled=True),
+        _step_on_sides(packed[None]),
         lax.all_gather(position[None], "dp", axis=0, tiled=True),
     )
     dp_index = jnp.arange(dp_count, dtype=jnp.int32)[:, None]

time: 582 us -> 620 us (1.065)
  blocking collectives: 246 us -> 332 us
  waiting for transfers between devices: 101 us -> 55.5 us
  local copies, waits for them, and re-layouts: 178 us -> 169 us
  starting transfers between devices: 9.69 us -> 16.9 us
    all_gather x1, blocking collectives: 8.96 us -> 94.8 us  [body(): lax.all_gather(position[None], 'dp', axis=0, tiled=True)]
    all_gather x1 -> x0, waiting for transfers between devices: 44.1 us -> none  [body(): lax.all_gather(packed[None], 'dp', axis=0, tiled=True)]
    all_gather x1 -> x0, local copies, waits for them, and re-layouts: 16.4 us -> none  [body(): lax.all_gather(packed[None], 'dp', axis=0, tiled=True)]
    another operation x0 -> x2, local copies, waits for them, and re-layouts: none -> 7.62 us  [the longest x1 6.54 us: _step_on_sides(): jnp.stack(lax.psum(1, 'dp') * [local_x], axis=0)]
    all_to_all x0 -> x1, starting transfers between devices: none -> 7.27 us  [_step_on_sides(): lax.all_to_all(jnp.stack(lax.psum(1, 'dp') * [local_x], axis=0), 'dp', 0, 0)]
  transfers between devices with their start and end apart: 3 -> 3, of which waited for: 3 -> 2; matrix products, arithmetic and copies ran while one was open for 3% -> 2% of each run, Pallas kernels for 0% -> 0%
where the time goes in v1:
time: 620 us; the launch traced here: 618 us
  blocking collectives  332 us (54%)
  local copies, waits for them, and re-layouts  169 us (27%)
  waiting for transfers between devices  55.5 us (9%)
  matrix products  28 us (5%)
  starting transfers between devices  16.9 us (3%)
  between operations  14.2 us (2%)
    all_to_all x1, blocking collectives, body(): lax.all_to_all(outgoing.reshape(lang_count, dp_count * per_peer, 2, feat_...  237 us
    scatter x1, local copies, waits for them, and re-layouts, body(): outgoing.at[target.reshape(-1)]  128 us
    all_gather x1, blocking collectives, body(): lax.all_gather(position[None], 'dp', axis=0, tiled=True)  94.8 us
    reduce_scatter x1, waiting for transfers between devices, body(): lax.psum_scatter(partial_dx.astype(jnp.bfloat16), 'dp', scatter_dimension...  41.6 us
    all_to_all x1, waiting for transfers between devices, body(): lax.all_to_all(summed.astype(jnp.bfloat16), 'lang', split_axis=0, concat_...  13.9 us
    all_to_all x1, local copies, waits for them, and re-layouts, body(): lax.all_to_all(outgoing.reshape(lang_count, dp_count * per_peer, 2, feat_...  12.9 us
  transfers between devices with their start and end apart: 3, of which 2 were waited for; matrix products, arithmetic and copies ran while one was open for 2% of the time, Pallas kernels for 0%

profile of v1, /device:TPU:25, one launch (start us, length us, event | category | flops | bytes accessed | tf_op | source)
XLA Modules:
  0.0 617.9 jit_solution(6312208255353102019)
XLA Ops:
  7.2 0.0 copy-start
  7.2 1.4 pad_maximum_fusion
  8.6 1.1 copy.40
  9.7 6.5 %stack.15 = bf16[8,1,128,2,2048]{4,3,2,1,0:T(2,128)(2,1)} broadcast(bf16[128,2,2048]{2,1,0:T(2,128)(2,1)S(1)} %copy.40), dimensions={2,3,4} | broadcast | bytes 9437184 | tf_op jit(solution)/shard_map/stack | solution.py:11
  16.3 0.0 copy-start.2
  16.3 0.0 copy-start.3
  16.3 0.0 copy-start.5
  16.3 7.3 %all-to-all-start = ((bf16[8,1,128,2,2048]{4,3,2,1,0:T(2,128)(2,1)}), bf16[8,1,128,2,2048]{4,3,2,1,0:T(2,128)(2,1)}, u32[]{:S(2)}, u32[]{:S(2)}) async-start(bf16[8,1,128,2,2048]{4,3,2,1,0:T(2,128)(2,1)} %stack.15), calls=%async_computation | async-start | bytes 16777216 | tf_op jit(solution)/shard_map/all_to_all | solution.py:11
  23.5 0.0 reduce-scatter.2.cloned.1.call-start
  23.5 0.0 copy-done.2
  23.5 0.0 copy-done.3
  23.6 0.1 select_reduce_fusion
  23.7 0.0 copy-done.5
  23.7 0.2 select_reduce_fusion.2
  23.8 0.1 fusion.23
  23.9 0.2 reduce_window_sum.11
  24.1 0.2 select_reduce_fusion.1
  24.3 94.8 %all-gather.1 = s32[8,1,128]{2,1,0:T(1,128)S(1)} all-gather(s32[1,1,128]{2,1,0:T(1,128)S(1)} %fusion.34), channel_id=2, replica_groups=mesh['dp'=8,'lang'=32] {'dp'}, dimensions={0}, use_global_device_ids=true | all-gather | bytes 4608 | tf_op jit(solution)/shard_map/all_gather | solution.py:65
  119.1 0.4 rem.15
  119.5 0.1 fusion.26
  119.6 0.0 all-to-all-done
  119.6 6.6 %broadcast_in_dim.6 = bf16[1280,2,2048]{2,1,0:T(2,128)(2,1)} broadcast(bf16[]{:T(256)} %constant.15.clone.1), dimensions={} | broadcast | bytes 10485762 | tf_op jit(solution)/shard_map/broadcast_in_dim | solution.py:69
  126.2 127.9 %scatter_fusion = bf16[1280,2,2048]{2,1,0:T(2,128)(2,1)} fusion(bf16[1280,2,2048]{2,1,0:T(2,128)(2,1)} %broadcast_in_dim.6, s32[1024]{0:T(1024)S(1)} %bitcast.75, bf16[1024,2,2048]{2,1,0:T(2,128)(2,1)} %bitcast.11), kind=kCustom, calls=%fused_computation.1 | custom fusion | bytes 25169920 | tf_op jit(solution)/shard_map/scatter | solution.py:70
  254.1 236.9 %all_to_all.15 = bf16[32,40,2,2048]{3,2,1,0:T(2,128)(2,1)} all-to-all(bf16[32,40,2,2048]{3,2,1,0:T(2,128)(2,1)} %bitcast.63), channel_id=1, replica_groups=mesh['dp'=8,'lang'=32] {'lang'}, dimensions={0} | all-to-all | bytes 20971520 | tf_op jit(solution)/shard_map/all_to_all | solution.py:71
  491.0 12.9 %copy.41 = bf16[32,40,2,2048]{3,1,0,2:T(8,128)(2,1)} copy(bf16[32,40,2,2048]{3,2,1,0:T(2,128)(2,1)} %all_to_all.15) | data formatting | bytes 20971520 | tf_op jit(solution)/shard_map/all_to_all | solution.py:71
  503.9 0.0 copy-done
  503.9 0.0 copy-start.1
  503.9 0.0 copy-start.4
  503.9 5.2 fusion.3
  509.1 0.0 copy-start.6
  509.2 1.5 copy-done.6
  510.6 0.0 copy-done.1
  510.6 0.0 copy-done.4
  510.6 4.3 fusion.5
  514.9 1.6 dot_general.19
  516.5 4.9 convolution_convert_fusion
  521.4 5.2 copy.43
  526.7 0.0 reduce-scatter.2.cloned.1.call-update
  526.7 41.6 %reduce-scatter.2.cloned.1.call-done = bf16[32,1,5,2048]{3,0,2,1:T(8,128)(2,1)} async-done(((bf16[32,8,5,2048]{3,0,2,1:T(8,128)(2,1)}), bf16[32,1,5,2048]{3,0,2,1:T(8,128)(2,1)}) %reduce-scatter.2.cloned.1.call-update) | async-done | bytes 655376 | tf_op jit(solution)/shard_map/reduce_scatter | solution.py:83
  568.3 2.4 copy.44
  570.8 9.6 %all-to-all-start.2 = ((bf16[32,5,2048]{2,1,0:T(8,128)(2,1)}), bf16[32,5,2048]{2,1,0:T(8,128)(2,1)}, u32[]{:S(2)}, u32[]{:S(2)}) async-start(bf16[32,5,2048]{2,1,0:T(8,128)(2,1)} %copy.44), calls=%async_computation.3 | async-start | bytes 2097152 | tf_op jit(solution)/shard_map/all_to_all | solution.py:87
  580.4 0.0 copy-start.7
  580.4 6.7 %fusion.9 = bf16[1,512,2048]{2,1,0:T(8,128)(2,1)} fusion(bf16[1280,512]{1,0:T(8,128)(2,1)S(1)} %fusion.5, bf16[1280,2,2048]{2,0,1:T(8,128)(2,1)} %bitcast.65), kind=kOutput, calls=%fused_computation.16 | convolution fusion | flops 2685403136 | bytes 8650752 | tf_op jit(solution)/shard_map/dot_general | solution.py:34
  587.2 0.0 copy-done.7
  587.2 6.8 %fusion.8 = bf16[1,512,2048]{2,1,0:T(8,128)(2,1)} fusion(bf16[1280,2,2048]{2,0,1:T(8,128)(2,1)} %bitcast.66, f32[1280,512]{1,0:T(8,128)S(1)} %copy-done.7), kind=kOutput, calls=%fused_computation.15 | convolution fusion | flops 2691301376 | bytes 9961472 | tf_op jit(solution)/shard_map/dot_general | solution.py:33
  594.0 13.9 %all-to-all-done.2 = bf16[32,5,2048]{2,1,0:T(8,128)(2,1)} async-done(((bf16[32,5,2048]{2,1,0:T(8,128)(2,1)}), bf16[32,5,2048]{2,1,0:T(8,128)(2,1)}, u32[]{:S(2)}, u32[]{:S(2)}) %all-to-all-start.2) | async-done | bytes 655392 | tf_op jit(solution)/shard_map/all_to_all | solution.py:87
  607.9 1.5 reshape.108
  609.4 1.7 gather_fusion
  (6 shorter events, 0.0 us)
Async XLA Ops:
  7.2 496.7 %copy-start = (bf16[1,512,2048]{2,1,0:T(8,128)(2,1)S(1)}, bf16[1,512,2048]{2,1,0:T(8,128)(2,1)}, u32[]{:S(2)}) copy-start(bf16[1,512,2048]{2,1,0:T(8,128)(2,1)} %param.12) | copy-start | bytes 6291460
  16.3 7.3 %copy-start.2 = (s32[200]{0:T(256)S(1)}, s32[200]{0:T(256)}, u32[]{:S(2)}) copy-start(s32[200]{0:T(256)} %param.10) | copy-start | bytes 2404
  16.3 7.3 %copy-start.3 = (s32[128]{0:T(128)S(1)}, s32[128]{0:T(128)}, u32[]{:S(2)}) copy-start(s32[128]{0:T(128)} %param.9) | copy-start | bytes 1540
  16.3 7.4 %copy-start.5 = (s32[32]{0:T(128)S(1)}, s32[32]{0:T(128)}, u32[]{:S(2)}) copy-start(s32[32]{0:T(128)} %param.11) | copy-start | bytes 388
  16.3 103.3 %all-to-all-start = ((bf16[8,1,128,2,2048]{4,3,2,1,0:T(2,128)(2,1)}), bf16[8,1,128,2,2048]{4,3,2,1,0:T(2,128)(2,1)}, u32[]{:S(2)}, u32[]{:S(2)}) async-start(bf16[8,1,128,2,2048]{4,3,2,1,0:T(2,128)(2,1)} %stack.15), calls=%async_computation | async-start | bytes 16777216 | tf_op jit(solution)/shard_map/all_to_all | solution.py:11
  23.5 544.8 %reduce-scatter.2.cloned.1.call-start = ((), (), s32[]{:S(2)}) async-start(), calls=%async_computation.4 | async-start | bytes 5898240 | tf_op jit(solution)/shard_map/reduce_scatter | solution.py:83
  503.9 6.7 %copy-start.1 = (bf16[32,40,2,2048]{3,1,0,2:T(8,128)(2,1)S(1)}, bf16[32,40,2,2048]{3,1,0,2:T(8,128)(2,1)}, u32[]{:S(2)}) copy-start(bf16[32,40,2,2048]{3,1,0,2:T(8,128)(2,1)} %copy.41) | copy-start | bytes 31457284
  503.9 6.7 %copy-start.4 = (bf16[1,512,2048]{2,1,0:T(8,128)(2,1)S(1)}, bf16[1,512,2048]{2,1,0:T(8,128)(2,1)}, u32[]{:S(2)}) copy-start(bf16[1,512,2048]{2,1,0:T(8,128)(2,1)} %param.13) | copy-start | bytes 6291460
  509.1 1.5 copy-start.6
  570.8 37.1 %all-to-all-start.2 = ((bf16[32,5,2048]{2,1,0:T(8,128)(2,1)}), bf16[32,5,2048]{2,1,0:T(8,128)(2,1)}, u32[]{:S(2)}, u32[]{:S(2)}) async-start(bf16[32,5,2048]{2,1,0:T(8,128)(2,1)} %copy.44), calls=%async_computation.3 | async-start | bytes 2097152 | tf_op jit(solution)/shard_map/all_to_all | solution.py:87
  580.4 6.8 %copy-start.7 = (f32[1280,512]{1,0:T(8,128)S(1)}, f32[1280,512]{1,0:T(8,128)}, u32[]{:S(2)}) copy-start(f32[1280,512]{1,0:T(8,128)} %copy-done.6) | copy-start | bytes 7864324
Sparse Core Ops, SparseCore 0:
  526.8 41.4 reduce-scatter.1
